TPU v7x, 512 devices: a whole 4x4x16 slice. The times are simulated.
512 devices in a mesh: seq: 32 (over x, z_lo), expert: 8 (over z_hi, y), mp: 2 (over core).
Axes of the slice: x: 4, y: 4, z: 16 (z_hi: 2, z_lo: 8; z = z_hi * 8 + z_lo), core: 2. Of those that a mesh axis runs over, the one named last changes fastest.
Arguments:
- queries: bfloat16 [8, 32, 128, 4096], P('expert', 'seq', None, 'mp'), may hold values from -6 to 6
- out_grad: bfloat16 [8, 32, 128, 4096], P('expert', 'seq', None, 'mp'), may hold values from -6 to 6
- prompt_kv: bfloat16 [8, 1024, 2, 256], P('expert', 'seq', None, 'mp'), may hold values from -6 to 6
- resp_kv: bfloat16 [8, 32, 128, 2, 256], P('expert', 'seq', None, None, 'mp'), may hold values from -6 to 6
- lengths: int32 [8, 32], P('expert', 'seq'), may hold values from 1 to 128, 3072 in all within a row
- grads: bfloat16 [8, 32, 128, 2048], P('expert', 'seq'), may hold values from -6 to 6
- routes: int32 [8, 32, 128, 8], P('expert', 'seq'), may hold values from 0 to 127, all different within a row; in each aligned block of 128 rows (0 to 127, 128 to 255, ..., all dimensions but the last counted through in order) at most 16 rows name the same one
- gates: float32 [8, 32, 128, 8], P('expert', 'seq'), may hold values from 0.1 to 1
- down_weight: bfloat16 [8, 1536, 2048], P('expert', 'mp'), may hold values from -0.125 to 0.125
Outputs:
- prompt_dkv: float32 [8, 1024, 2, 256], P('expert', 'seq', None, 'mp')
- resp_dkv: float32 [8, 32, 128, 2, 256], P('expert', 'seq', None, None, 'mp')
- expert_grad: bfloat16 [32, 8, 8, 16, 1536], P('seq', None, 'expert', None, 'mp')
Inputs may be any that keep to these rules, and one draw needn't show every extreme that they name: `routes`: the 8 experts of a token differ; among the rows of one device no expert is named by more than 16 rows.
All inputs are finite; a program needn't handle non-finite values. No bound on the sum of `lengths` on one device may be relied on, other than what follows from the above.
Results may differ from a plain program's by a relative error of at most 0.0049.
Values may be sent and summed in bfloat16 or wider, within the bound.
A program may use at most 64 MiB of HBM per device.

v0:
```python
import jax
import jax.numpy as jnp
from jax import lax
from jax.sharding import PartitionSpec as P

HD = 128


def local(queries, out_grad, prompt_kv, resp_kv, lengths, grads, routes, gates, down_weight):
    query_rows = queries[0, 0]
    row_count = query_rows.shape[0]
    kv_heads = resp_kv.shape[-1] // HD
    q_heads = query_rows.shape[-1] // HD
    group_size = q_heads // kv_heads
    score_scale = HD ** (-0.5)
    query_heads = query_rows.reshape(row_count, kv_heads, group_size, HD)
    gathered = lax.all_gather(prompt_kv, "seq", axis=1, tiled=True)
    prompt_len = gathered.shape[1]
    key_rows = jnp.concatenate([gathered[0, :, 0], resp_kv[0, 0, :, 0]], 0).reshape(
        -1, kv_heads, HD
    )
    value_rows = jnp.concatenate([gathered[0, :, 1], resp_kv[0, 0, :, 1]], 0).reshape(
        -1, kv_heads, HD
    )
    key_total = key_rows.shape[0]
    length = lengths[0, 0]
    position = jnp.arange(row_count)
    allowed = jnp.concatenate(
        [jnp.ones((row_count, prompt_len), jnp.bool_), position[None, :] <= position[:, None]], 1
    )
    scores = (
        jnp.einsum("icgd,jcd->cgij", query_heads, key_rows, preferred_element_type=jnp.float32)
        * score_scale
    )
    scores = jnp.where(allowed, scores, -jnp.inf)
    numerators = jnp.exp(scores - jnp.max(scores, -1, keepdims=True))
    attention = numerators / jnp.sum(numerators, -1, keepdims=True)
    attention_low = attention.astype(jnp.bfloat16)
    grad_out = out_grad[0, 0]
    grad_rows = jnp.where((position < length)[:, None], grad_out, jnp.zeros_like(grad_out))
    grad_heads = grad_rows.reshape(row_count, kv_heads, group_size, HD)
    grad_probs = jnp.einsum(
        "icgd,jcd->cgij", grad_heads, value_rows, preferred_element_type=jnp.float32
    )
    row_delta = jnp.sum(attention * grad_probs, -1, keepdims=True)
    grad_low = (attention * (grad_probs - row_delta) * score_scale).astype(jnp.bfloat16)
    grad_keys = jnp.einsum(
        "cgij,icgd->jcd", grad_low, query_heads, preferred_element_type=jnp.float32
    )
    grad_values = jnp.einsum(
        "cgij,icgd->jcd", attention_low, grad_heads, preferred_element_type=jnp.float32
    )
    every_term = jnp.stack(
        [
            grad_keys.reshape(key_total, kv_heads * HD),
            grad_values.reshape(key_total, kv_heads * HD),
        ],
        1,
    )
    prompt_part = lax.psum_scatter(every_term[:prompt_len], "seq", scatter_dimension=0, tiled=True)
    own_part = every_term[prompt_len:]
    token_rows = grads[0, 0]
    route_ids = routes[0, 0]
    gate_rows = gates[0, 0]
    local_experts = down_weight.shape[0]
    expert_devices = lax.axis_size("expert")
    capacity = row_count // 8
    expert_ids = jnp.arange(local_experts * expert_devices)
    matches = route_ids[:, :, None] == expert_ids[None, None, :]
    named_rows = jnp.any(matches, 1)
    valid_rows = (position < length).astype(jnp.float32)
    route_weight = (
        jnp.sum(jnp.where(matches, gate_rows[:, :, None], jnp.zeros_like(gate_rows[:, :, None])), 1)
        * valid_rows[:, None]
    )
    slot_index = jnp.cumsum(named_rows.astype(jnp.int32), 0) - 1
    selection = named_rows[:, :, None] & (
        slot_index[:, :, None] == jnp.arange(capacity)[None, None, :]
    )
    picked = jnp.einsum(
        "ixc,id->xcd",
        selection.astype(jnp.bfloat16),
        token_rows,
        preferred_element_type=jnp.float32,
    )
    slot_gate = jnp.einsum(
        "ixc,ix->xc", selection.astype(jnp.float32), route_weight, precision=lax.Precision.HIGHEST
    )
    outgoing = (
        (picked * slot_gate[:, :, None])
        .astype(jnp.bfloat16)
        .reshape(expert_devices, local_experts, capacity, token_rows.shape[1])
    )
    expert_grad = jnp.einsum(
        "sxcd,xfd->sxcf",
        lax.all_to_all(outgoing, "expert", split_axis=0, concat_axis=0, tiled=True),
        down_weight,
        preferred_element_type=jnp.float32,
    ).astype(jnp.bfloat16)
    return (prompt_part[None], own_part[None, None], expert_grad[None])


def solution(mesh):
    placed = (
        P("expert", "seq", None, "mp"),
        P("expert", "seq", None, "mp"),
        P("expert", "seq", None, "mp"),
        P("expert", "seq", None, None, "mp"),
        P("expert", "seq"),
        P("expert", "seq", None, None),
        P("expert", "seq", None, None),
        P("expert", "seq", None, None),
        P("expert", "mp", None),
    )
    return jax.shard_map(
        local,
        mesh=mesh,
        in_specs=placed,
        out_specs=(
            P("expert", "seq", None, "mp"),
            P("expert", "seq", None, None, "mp"),
            P("seq", None, "expert", None, "mp"),
        ),
        check_vma=False,
    )
```

profile of v0, /device:TPU:8, one launch (start us, length us, event | category | flops | bytes accessed | tf_op | source)
XLA Modules:
  0.0 430.9 jit_solution(1173876097495905706)
XLA Ops:
  7.2 0.0 copy-start
  8.0 0.5 iota_compare_fusion.3
  8.5 0.7 fusion.49
  9.2 0.1 copy.54
  9.3 0.2 reduce_window_sum.11
  9.5 0.7 select_reduce_fusion
  10.3 0.2 fusion.44
  10.5 2.1 fusion.21
  12.6 18.2 %all-to-all-start = ((bf16[8,1,16,2048]{3,2,1,0:T(8,128)(2,1)}), bf16[8,1,16,2048]{3,2,1,0:T(8,128)(2,1)}, u32[]{:S(2)}, u32[]{:S(2)}) async-start(bf16[8,1,16,2048]{3,2,1,0:T(8,128)(2,1)} %fusion.21), calls=%async_computation.1 | async-start | bytes 1048576 | tf_op jit(solution)/shard_map/all_to_all | solution.py:96
  30.8 0.0 reduce-scatter.2.cloned.1.call-start
  30.8 1.0 fusion.59
  31.8 0.7 copy.45
  32.5 134.5 %all_gather.3 = bf16[1,1024,2,128]{3,1,2,0:T(8,128)(2,1)S(1)} all-gather(bf16[1,32,2,128]{3,1,2,0:T(8,128)(2,1)S(1)} %copy.45), channel_id=1, replica_groups=mesh['seq'=32,'expert'=8,'mp'=2] {'seq'}, dimensions={1}, use_global_device_ids=true | all-gather | bytes 540672 | tf_op jit(solution)/shard_map/all_gather | solution.py:17
  167.0 0.7 slice_bitcast_fusion.1
  167.8 1.9 copy.68
  169.7 2.0 copy.64
  171.7 1.1 select_bitcast_fusion
  172.9 0.1 copy.69
  173.1 0.0 copy-start.4
  173.1 0.0 copy-start.6
  173.1 2.5 fusion.60
  175.6 1.2 fusion.5
  176.9 0.0 copy-done.4
  176.9 0.0 copy-done.6
  176.9 0.0 copy-start.5
  176.9 1.6 fusion.17
  178.5 0.0 copy-start.2
  178.5 0.0 copy-done.5
  178.5 0.0 copy-start.1
  178.5 2.2 fusion
  180.8 0.0 copy-done.1
  180.8 2.7 fusion.14
  183.5 0.0 copy-done.2
  183.5 0.0 copy-start.3
  183.5 0.8 copy-done.3
  184.3 1.1 fusion.28
  185.4 0.0 reduce-scatter.2.cloned.1.call-update
  185.4 0.9 fusion.42
  186.3 0.8 copy.58
  187.0 0.0 all-to-all-done
  187.0 0.0 copy-done
  187.0 2.9 fusion.25
  189.9 232.7 %reduce-scatter.2.cloned.1.call-done = f32[32,2,128]{2,0,1:T(8,128)} async-done(((f32[1024,2,128]{2,0,1:T(8,128)}), f32[32,2,128]{2,0,1:T(8,128)}) %reduce-scatter.2.cloned.1.call-update) | async-done | bytes 32784 | tf_op jit(solution)/shard_map/reduce_scatter | solution.py:60
  422.7 1.4 copy.57
  (7 shorter events, 0.1 us)
Async XLA Ops:
  7.2 179.9 %copy-start = (bf16[1,768,2048]{2,1,0:T(8,128)(2,1)S(1)}, bf16[1,768,2048]{2,1,0:T(8,128)(2,1)}, u32[]{:S(2)}) copy-start(bf16[1,768,2048]{2,1,0:T(8,128)(2,1)} %param.17) | copy-start | bytes 9437188
  12.6 174.4 %all-to-all-start = ((bf16[8,1,16,2048]{3,2,1,0:T(8,128)(2,1)}), bf16[8,1,16,2048]{3,2,1,0:T(8,128)(2,1)}, u32[]{:S(2)}, u32[]{:S(2)}) async-start(bf16[8,1,16,2048]{3,2,1,0:T(8,128)(2,1)} %fusion.21), calls=%async_computation.1 | async-start | bytes 1048576 | tf_op jit(solution)/shard_map/all_to_all | solution.py:96
  30.8 391.9 %reduce-scatter.2.cloned.1.call-start = ((), (), s32[]{:S(2)}) async-start(), calls=%async_computation.2 | async-start | bytes 1081344 | tf_op jit(solution)/shard_map/reduce_scatter | solution.py:60
  173.1 3.8 copy-start.4
  173.1 3.8 copy-start.6
  176.9 1.6 copy-start.5
  178.5 5.0 %copy-start.2 = (f32[1152,1,128]{2,0,1:T(8,128)}, f32[1152,1,128]{2,0,1:T(8,128)S(1)}, u32[]{:S(2)}) copy-start(f32[1152,1,128]{2,0,1:T(8,128)S(1)} %fusion.17) | copy-start | bytes 1769476
  178.5 2.3 copy-start.1
  183.5 0.8 copy-start.3
Sparse Core Ops, SparseCore 0:
  185.5 237.1 reduce-scatter.1
where the time goes:
time: 432 us; the launch traced here: 431 us
  waiting for transfers between devices  233 us (54%)
  blocking collectives  134 us (31%)
  starting transfers between devices  18.2 us (4%)
  between operations  15 us (3%)
  matrix products  14.2 us (3%)
  local copies, waits for them, and re-layouts  9.8 us (2%)
  other arithmetic  6.48 us (2%)
    reduce_scatter x1, waiting for transfers between devices, local(): lax.psum_scatter(every_term[:prompt_len], 'seq', scatter_dimension=0, til...  233 us
    all_gather x1, blocking collectives, local(): gathered = lax.all_gather(prompt_kv, 'seq', axis=1, tiled=True)  134 us
    all_to_all x1, starting transfers between devices, local(): lax.all_to_all(outgoing, 'expert', split_axis=0, concat_axis=0, tiled=True)  18.2 us
  transfers between devices with their start and end apart: 2, of which 1 were waited for; matrix products, arithmetic and copies ran while one was open for 5% of the time, Pallas kernels for 0%

commit v1 on v0

--- a/solution.py
+++ b/solution.py
@@ -14,7 +14,9 @@
     group_size = q_heads // kv_heads
     score_scale = HD ** (-0.5)
     query_heads = query_rows.reshape(row_count, kv_heads, group_size, HD)
-    gathered = lax.all_gather(prompt_kv, "seq", axis=1, tiled=True)
+    gathered = jnp.concatenate(
+        lax.all_to_all(jnp.stack([prompt_kv] * lax.axis_size("seq")), "seq", 0, 0), axis=1
+    )
     prompt_len = gathered.shape[1]
     key_rows = jnp.concatenate([gathered[0, :, 0], resp_kv[0, 0, :, 0]], 0).reshape(
         -1, kv_heads, HD

time: 432 us -> 328 us (0.76)
  blocking collectives: 134 us -> 0 us
  waiting for transfers between devices: 233 us -> 254 us
  starting transfers between devices: 18.2 us -> 26.2 us
    all_gather x1 -> x0, blocking collectives: 134 us -> none  [local(): gathered = lax.all_gather(prompt_kv, 'seq', axis=1, tiled=True)]
    all_to_all x0 -> x1, waiting for transfers between devices: none -> 18.2 us  [local(): lax.all_to_all(jnp.stack([prompt_kv] * lax.axis_size('seq')), 'seq', 0, 0)]
    all_to_all x0 -> x1, starting transfers between devices: none -> 15.5 us  [local(): lax.all_to_all(jnp.stack([prompt_kv] * lax.axis_size('seq')), 'seq', 0, 0)]
    all_to_all x1, waiting for transfers between devices: 0.01 us -> 9.4 us  [local(): lax.all_to_all(outgoing, 'expert', split_axis=0, concat_axis=0, tiled=True)]
    all_to_all x1, starting transfers between devices: 18.2 us -> 10.7 us  [local(): lax.all_to_all(outgoing, 'expert', split_axis=0, concat_axis=0, tiled=True)]
    reduce_scatter x1, waiting for transfers between devices: 233 us -> 227 us  [local(): lax.psum_scatter(every_term[:prompt_len], 'seq', scatter_dimension=0, til...]
  transfers between devices with their start and end apart: 2 -> 3, of which waited for: 1 -> 3; matrix products, arithmetic and copies ran while one was open for 5% -> 9% of each run, Pallas kernels for 0% -> 0%
where the time goes in v1:
time: 328 us; the launch traced here: 327 us
  waiting for transfers between devices  254 us (77%)
  starting transfers between devices  26.2 us (8%)
  between operations  14.9 us (5%)
  matrix products  14 us (4%)
  local copies, waits for them, and re-layouts  12 us (4%)
  other arithmetic  5.96 us (2%)
    reduce_scatter x1, waiting for transfers between devices, local(): lax.psum_scatter(every_term[:prompt_len], 'seq', scatter_dimension=0, til...  227 us
    all_to_all x1, waiting for transfers between devices, local(): lax.all_to_all(jnp.stack([prompt_kv] * lax.axis_size('seq')), 'seq', 0, 0)  18.2 us
    all_to_all x1, starting transfers between devices, local(): lax.all_to_all(jnp.stack([prompt_kv] * lax.axis_size('seq')), 'seq', 0, 0)  15.5 us
    all_to_all x1, starting transfers between devices, local(): lax.all_to_all(outgoing, 'expert', split_axis=0, concat_axis=0, tiled=True)  10.7 us
    all_to_all x1, waiting for transfers between devices, local(): lax.all_to_all(outgoing, 'expert', split_axis=0, concat_axis=0, tiled=True)  9.4 us
  transfers between devices with their start and end apart: 3, of which 3 were waited for; matrix products, arithmetic and copies ran while one was open for 9% of the time, Pallas kernels for 0%

profile of v1, /device:TPU:8, one launch (start us, length us, event | category | flops | bytes accessed | tf_op | source)
XLA Modules:
  0.0 327.4 jit_solution(1892655159648154)
XLA Ops:
  7.2 0.0 copy-start
  7.2 0.9 copy.46
  8.1 0.9 stack.4
  9.0 15.5 %all-to-all-start = ((bf16[32,1,32,2,128]{4,2,3,1,0:T(8,128)(2,1)}), bf16[32,1,32,2,128]{4,2,3,1,0:T(8,128)(2,1)}, u32[]{:S(2)}, u32[]{:S(2)}) async-start(bf16[32,1,32,2,128]{4,2,3,1,0:T(8,128)(2,1)} %stack.4), calls=%async_computation | async-start | bytes 1048576 | tf_op jit(solution)/shard_map/all_to_all | solution.py:18
  24.5 1.9 copy.70
  27.1 2.0 copy.66
  29.1 1.1 select_bitcast_fusion
  30.3 0.9 copy.71
  31.2 0.7 fusion.49
  31.9 0.1 copy.56
  32.0 0.2 reduce_window_sum.11
  32.3 0.7 select_reduce_fusion
  33.0 0.2 fusion.44
  33.2 2.1 fusion.21
  35.3 1.0 fusion.59
  36.4 18.2 %all-to-all-done = bf16[32,1,32,2,128]{4,2,3,1,0:T(8,128)(2,1)} async-done(((bf16[32,1,32,2,128]{4,2,3,1,0:T(8,128)(2,1)}), bf16[32,1,32,2,128]{4,2,3,1,0:T(8,128)(2,1)}, u32[]{:S(2)}, u32[]{:S(2)}) %all-to-all-start) | async-done | bytes 524320 | tf_op jit(solution)/shard_map/all_to_all | solution.py:18
  54.7 10.7 %all-to-all-start.1 = ((bf16[8,1,16,2048]{3,2,1,0:T(8,128)(2,1)}), bf16[8,1,16,2048]{3,2,1,0:T(8,128)(2,1)}, u32[]{:S(2)}, u32[]{:S(2)}) async-start(bf16[8,1,16,2048]{3,2,1,0:T(8,128)(2,1)} %fusion.21), calls=%async_computation.2 | async-start | bytes 1048576 | tf_op jit(solution)/shard_map/all_to_all | solution.py:98
  65.3 0.0 reduce-scatter.2.cloned.1.call-start
  65.3 1.1 copy.47
  66.4 0.0 copy-start.5
  66.5 2.5 fusion.60
  69.0 1.2 fusion.5
  70.2 0.0 copy-done.5
  70.2 0.0 copy-start.1
  70.3 2.1 fusion
  72.3 0.0 copy-done.1
  72.3 0.0 copy-start.4
  72.4 2.6 fusion.14
  74.9 0.0 copy-start.2
  74.9 0.0 copy-done.4
  75.0 1.6 fusion.17
  76.5 0.0 copy-done.2
  76.6 0.0 copy-start.3
  76.6 0.8 copy-done.3
  77.4 1.1 fusion.28
  78.4 0.0 reduce-scatter.2.cloned.1.call-update
  78.5 9.4 %all-to-all-done.1 = bf16[8,1,16,2048]{3,2,1,0:T(8,128)(2,1)} async-done(((bf16[8,1,16,2048]{3,2,1,0:T(8,128)(2,1)}), bf16[8,1,16,2048]{3,2,1,0:T(8,128)(2,1)}, u32[]{:S(2)}, u32[]{:S(2)}) %all-to-all-start.1) | async-done | bytes 524320 | tf_op jit(solution)/shard_map/all_to_all | solution.py:98
  87.9 0.0 copy-done
  87.9 2.9 fusion.25
  90.8 0.9 fusion.42
  91.7 0.8 copy.60
  92.4 226.7 %reduce-scatter.2.cloned.1.call-done = f32[32,2,128]{2,0,1:T(8,128)} async-done(((f32[1024,2,128]{2,0,1:T(8,128)}), f32[32,2,128]{2,0,1:T(8,128)}) %reduce-scatter.2.cloned.1.call-update) | async-done | bytes 32784 | tf_op jit(solution)/shard_map/reduce_scatter | solution.py:62
  319.1 1.4 copy.59
  (9 shorter events, 0.2 us)
Async XLA Ops:
  7.2 80.7 %copy-start = (bf16[1,768,2048]{2,1,0:T(8,128)(2,1)S(1)}, bf16[1,768,2048]{2,1,0:T(8,128)(2,1)}, u32[]{:S(2)}) copy-start(bf16[1,768,2048]{2,1,0:T(8,128)(2,1)} %param.17) | copy-start | bytes 9437188
  9.0 45.7 %all-to-all-start = ((bf16[32,1,32,2,128]{4,2,3,1,0:T(8,128)(2,1)}), bf16[32,1,32,2,128]{4,2,3,1,0:T(8,128)(2,1)}, u32[]{:S(2)}, u32[]{:S(2)}) async-start(bf16[32,1,32,2,128]{4,2,3,1,0:T(8,128)(2,1)} %stack.4), calls=%async_computation | async-start | bytes 1048576 | tf_op jit(solution)/shard_map/all_to_all | solution.py:18
  54.7 33.2 %all-to-all-start.1 = ((bf16[8,1,16,2048]{3,2,1,0:T(8,128)(2,1)}), bf16[8,1,16,2048]{3,2,1,0:T(8,128)(2,1)}, u32[]{:S(2)}, u32[]{:S(2)}) async-start(bf16[8,1,16,2048]{3,2,1,0:T(8,128)(2,1)} %fusion.21), calls=%async_computation.2 | async-start | bytes 1048576 | tf_op jit(solution)/shard_map/all_to_all | solution.py:98
  65.3 253.8 %reduce-scatter.2.cloned.1.call-start = ((), (), s32[]{:S(2)}) async-start(), calls=%async_computation.3 | async-start | bytes 1081344 | tf_op jit(solution)/shard_map/reduce_scatter | solution.py:62
  66.4 3.8 %copy-start.5 = (bf16[16,8,16,128]{3,2,1,0:T(8,128)(2,1)S(1)}, bf16[16,8,16,128]{3,2,1,0:T(8,128)(2,1)}, u32[]{:S(2)}) copy-start(bf16[16,8,16,128]{3,2,1,0:T(8,128)(2,1)} %copy.71) | copy-start | bytes 1572868
  70.2 2.1 copy-start.1
  72.3 2.6 copy-start.4
  74.9 1.6 copy-start.2
  76.6 0.8 copy-start.3
Sparse Core Ops, SparseCore 0:
  78.6 240.4 reduce-scatter.1
